TPU v7x, 32 devices: a whole 2x2x4 slice. The times are simulated.
32 devices in a mesh: grid: 8 (over y, x, core), pts: 4 (over z).
Axes of the slice: x: 2, y: 2, z: 4, core: 2. Of those that a mesh axis runs over, the one named last changes fastest.
Arguments:
- orbitals: bfloat16 [8192, 512], P(('grid', 'pts')), may hold values from -6 to 6
- point_rows: int32 [32, 4, 24], P(('grid', 'pts')), may hold values from 0 to 255, as said below
- point_count: int32 [32, 4], P(('grid', 'pts')), may hold values from 12 to 24, as said below
- potential: bfloat16 [3072, 4, 768], P('pts', None, 'grid'), may hold values from -0.004760742 to 0.004760742
- fitted_basis: bfloat16 [8192, 3072], P('grid', 'pts'), may hold values from -0.109375 to 0.109375
Outputs:
- updated: bfloat16 [8192, 512], P(('grid', 'pts'))
- projection: bfloat16 [3072, 512], P('pts')
Inputs may be any that keep to these rules, and one draw needn't show every extreme that they name: `point_count`: each source device has at least one owner with all 24 slots valid. `point_rows`: the listed rows of one source device are all different.
All inputs are finite; a program needn't handle non-finite values.
Results may differ from a plain program's by a relative error of at most 0.0055.
Values may be sent and summed in bfloat16 or wider, within the bound.
A program may use at most 128 MiB of HBM per device.

v0:
```python
import jax
import jax.numpy as jnp
from jax import lax
from jax.sharding import PartitionSpec as P


def on_device(orbitals, point_rows, point_count, potential, fitted_basis):
    width = orbitals.shape[1]
    owners = point_rows.shape[1]
    per_owner = point_rows.shape[2]
    picked = jnp.take(orbitals, point_rows[0], axis=0)
    valid_slot = lax.broadcasted_iota(jnp.int32, (owners, per_owner), 1) < point_count[0][:, None]
    picked = jnp.where(valid_slot[:, :, None], picked, jnp.zeros_like(picked))
    arrived = lax.all_to_all(picked, "pts", split_axis=0, concat_axis=0, tiled=True)
    slot_rows = arrived.reshape(owners * per_owner, width)
    own_points = lax.all_gather(slot_rows, "grid", axis=0, tiled=True)
    own_count = own_points.shape[0]
    pot_cols = potential.reshape(own_count, -1)
    piece = lax.all_gather(slot_rows, "pts", axis=0, tiled=True)
    pair_dens = jnp.dot(own_points, piece.T, preferred_element_type=jnp.float32)
    weighted = (pot_cols.astype(jnp.float32) * pair_dens).astype(jnp.bfloat16)
    proj_part = jnp.dot(weighted, piece, preferred_element_type=jnp.float32)
    proj_share = lax.psum_scatter(proj_part, "grid", scatter_dimension=0, tiled=True).astype(
        jnp.bfloat16
    )
    projection = lax.all_gather(proj_share, "grid", axis=0, tiled=True)
    exchange = lax.psum_scatter(
        jnp.dot(fitted_basis, projection, preferred_element_type=jnp.float32),
        "pts",
        scatter_dimension=0,
        tiled=True,
    )
    updated = (orbitals.astype(jnp.float32) - exchange).astype(jnp.bfloat16)
    return (updated, projection)


def solution(mesh):
    in_specs = (
        P(("grid", "pts"), None),
        P(("grid", "pts"), None, None),
        P(("grid", "pts"), None),
        P("pts", None, "grid"),
        P("grid", "pts"),
    )
    out_specs = (P(("grid", "pts"), None), P("pts", None))
    return jax.shard_map(
        on_device, mesh=mesh, in_specs=in_specs, out_specs=out_specs, check_vma=False
    )
```

profile of v0, /device:TPU:0, one launch (start us, length us, event | category | flops | bytes accessed | tf_op | source)
XLA Modules:
  0.0 154.0 jit_solution(305977543143108675)
XLA Ops:
  7.2 0.0 copy-start
  7.2 0.0 copy-start.2
  7.2 0.0 reduce-scatter.3.cloned.1.call-start
  7.2 0.8 compare_select_fusion
  8.1 0.8 iota_compare_fusion
  8.8 0.1 reshape.70
  8.9 1.8 %gather_fusion = bf16[96,512]{1,0:T(8,128)(2,1)S(1)} fusion(bf16[256,512]{1,0:T(8,128)(2,1)} %param.5, s32[1024]{0:T(1024)S(1)} %pad_clamp_fusion), kind=kCustom, calls=%fused_computation | custom fusion | bytes 196992 | tf_op jit(solution)/shard_map/jit(_take)/gather | solution.py:11
  10.7 0.1 select_select_fusion
  10.8 12.0 %all_to_all.5 = bf16[4,24,512]{2,1,0:T(8,128)(2,1)S(1)} all-to-all(bf16[4,24,512]{2,1,0:T(8,128)(2,1)S(1)} %select_select_fusion), channel_id=1, replica_groups=mesh['grid'=8,'pts'=4] {'pts'}, dimensions={0} | all-to-all | bytes 196608 | tf_op jit(solution)/shard_map/all_to_all | solution.py:14
  22.8 10.4 %all_gather.9 = bf16[768,512]{1,0:T(8,128)(2,1)S(1)} all-gather(bf16[96,512]{1,0:T(8,128)(2,1)S(1)} %bitcast.20), channel_id=1, replica_groups=mesh['grid'=8,'pts'=4] {'grid'}, dimensions={0}, use_global_device_ids=true | all-gather | bytes 884736 | tf_op jit(solution)/shard_map/all_gather | solution.py:16
  33.2 15.3 %all_gather.10 = bf16[384,512]{1,0:T(8,128)(2,1)S(1)} all-gather(bf16[96,512]{1,0:T(8,128)(2,1)S(1)} %bitcast.21), channel_id=1, replica_groups=mesh['grid'=8,'pts'=4] {'pts'}, dimensions={0}, use_global_device_ids=true | all-gather | bytes 491520 | tf_op jit(solution)/shard_map/all_gather | solution.py:19
  48.5 0.0 copy-done.2
  48.5 2.2 %fusion.1 = f32[768,512]{1,0:T(8,128)} fusion(bf16[384,512]{1,0:T(8,128)(2,1)S(1)} %all_gather.10, bf16[768,512]{1,0:T(8,128)(2,1)S(1)} %all_gather.9, bf16[768,384]{0,1:T(8,128)(2,1)S(1)} %bitcast.22), kind=kOutput, calls=%fused_computation.4 | convolution fusion | flops 604864512 | bytes 3342336 | tf_op jit(solution)/shard_map/dot_general | solution.py:22
  50.6 0.0 reduce-scatter.3.cloned.1.call-update
  50.7 0.0 reduce-scatter.5.cloned.1.call-start
  50.7 36.0 %reduce-scatter.3.cloned.1.call-done = f32[96,512]{1,0:T(8,128)} async-done(((f32[768,512]{1,0:T(8,128)}), f32[96,512]{1,0:T(8,128)}) %reduce-scatter.3.cloned.1.call-update) | async-done | bytes 196624 | tf_op jit(solution)/shard_map/reduce_scatter | solution.py:23
  86.7 0.9 convert_element_type.22
  87.6 10.3 %all_gather.11 = bf16[768,512]{1,0:T(8,128)(2,1)S(1)} all-gather(bf16[96,512]{1,0:T(8,128)(2,1)S(1)} %convert_element_type.22), channel_id=1, replica_groups=mesh['grid'=8,'pts'=4] {'grid'}, dimensions={0}, use_global_device_ids=true | all-gather | bytes 884736 | tf_op jit(solution)/shard_map/all_gather | solution.py:26
  98.0 0.0 copy-done
  98.0 2.4 %convolution_bitcast_fusion = f32[1024,512]{0,1:T(8,128)} fusion(bf16[768,512]{1,0:T(8,128)(2,1)S(1)} %all_gather.11, bf16[1024,768]{1,0:T(8,128)(2,1)S(1)} %copy-done), kind=kOutput, calls=%fused_computation.1 | convolution fusion | flops 805306368 | bytes 4456448 | tf_op jit(solution)/shard_map/dot_general | solution.py:28
  100.3 0.0 copy-start.1
  100.3 0.0 reduce-scatter.5.cloned.1.call-update
  100.3 0.9 copy-done.1
  101.3 0.1 copy.7
  101.4 43.0 %reduce-scatter.5.cloned.1.call-done = f32[256,512]{0,1:T(8,128)} async-done(((f32[1024,512]{0,1:T(8,128)}), f32[256,512]{0,1:T(8,128)}) %reduce-scatter.5.cloned.1.call-update) | async-done | bytes 524304 | tf_op jit(solution)/shard_map/reduce_scatter | solution.py:27
  144.4 1.1 subtract_convert_fusion
  145.5 0.8 copy.8
  146.3 0.9 copy.10
  (1 shorter events, 0.0 us)
Async XLA Ops:
  7.2 90.8 %copy-start = (bf16[1024,768]{1,0:T(8,128)(2,1)S(1)}, bf16[1024,768]{1,0:T(8,128)(2,1)}, u32[]{:S(2)}) copy-start(bf16[1024,768]{1,0:T(8,128)(2,1)} %param.9) | copy-start | bytes 4718596
  7.2 41.3 %copy-start.2 = (bf16[768,4,96]{0,2,1:T(8,128)(2,1)S(1)}, bf16[768,4,96]{0,2,1:T(8,128)(2,1)}, u32[]{:S(2)}) copy-start(bf16[768,4,96]{0,2,1:T(8,128)(2,1)} %param.8) | copy-start | bytes 1769476
  7.2 79.5 %reduce-scatter.3.cloned.1.call-start = ((), (), s32[]{:S(2)}) async-start(), calls=%async_computation.3 | async-start | bytes 1769472 | tf_op jit(solution)/shard_map/reduce_scatter | solution.py:23
  50.7 93.7 %reduce-scatter.5.cloned.1.call-start = ((), (), s32[]{:S(2)}) async-start(), calls=%async_computation.4 | async-start | bytes 2621440 | tf_op jit(solution)/shard_map/reduce_scatter | solution.py:27
  100.3 0.9 copy-start.1
Sparse Core Ops, SparseCore 0:
  50.8 35.8 reduce-scatter.2
  100.5 43.8 reduce-scatter.4
where the time goes:
time: 154 us
  waiting for transfers between devices  79 us (51%)
  blocking collectives  48 us (31%)
  between operations  14.1 us (9%)
  local copies, waits for them, and re-layouts  4.65 us (3%)
  matrix products  4.51 us (3%)
  other arithmetic  3.75 us (2%)
    reduce_scatter x1, waiting for transfers between devices, on_device(): lax.psum_scatter(jnp.dot(fitted_basis, projection, preferred_element_type...  43 us
    reduce_scatter x1, waiting for transfers between devices, on_device(): lax.psum_scatter(proj_part, 'grid', scatter_dimension=0, tiled=True)  36 us
    all_gather x1, blocking collectives, on_device(): piece = lax.all_gather(slot_rows, 'pts', axis=0, tiled=True)  15.3 us
    all_to_all x1, blocking collectives, on_device(): lax.all_to_all(picked, 'pts', split_axis=0, concat_axis=0, tiled=True)  12 us
    all_gather x1, blocking collectives, on_device(): own_points = lax.all_gather(slot_rows, 'grid', axis=0, tiled=True)  10.4 us
    all_gather x1, blocking collectives, on_device(): projection = lax.all_gather(proj_share, 'grid', axis=0, tiled=True)  10.3 us
  transfers between devices with their start and end apart: 2, of which 2 were waited for; matrix products, arithmetic and copies ran while one was open for 0% of the time, Pallas kernels for 0%

commit v1 on v0

v1 whole, which is shorter than its diff:
```python
import functools

import jax
import jax.numpy as jnp
from jax import lax
from jax.experimental import pallas as pl
from jax.experimental.pallas import tpu as pltpu
from jax.sharding import PartitionSpec as P

MESH = pl.DeviceIdType.MESH
F32 = jnp.float32
BF16 = jnp.bfloat16
CORES = 2
HALVES = 2


def kernel(
    n_grid,
    n_pts,
    tile,
    orb_ref,
    rows_ref,
    count_ref,
    pot_ref,
    fit_ref,
    upd_ref,
    prj_ref,
    fit,
    pot_in,
    pot,
    piece,
    cols,
    own,
    part,
    sib_out,
    sib_in,
    chip_out,
    chip_in,
    proj,
    exch,
    z_out,
    z_in,
    load_sem,
    a_send,
    a_recv,
    c_send,
    c_recv,
    s_send,
    s_recv,
    d_send,
    d_recv,
    e_send,
    e_recv,
    up_send,
    up_recv,
    dn_send,
    dn_recv,
):
    g = lax.axis_index("grid")
    p = lax.axis_index("pts")
    chips = n_grid // CORES
    chip, core = g // CORES, g % CORES
    sib = chip * CORES + (1 - core)
    cap = piece.shape[2]
    rows_dev, width = orb_ref.shape
    half = width // HALVES
    own_count = own.shape[0]
    block = n_pts * cap
    tiles = own_count // tile

    def chip_at(r):
        return (chip + r) % chips

    def pts_at(r):
        return (p + r) % n_pts

    def rows_of(gg):
        return pl.ds(pl.multiple_of(gg * block, block), block)

    fit_copy = pltpu.make_async_copy(fit_ref, fit, load_sem.at[2])
    pot_copies = [
        pltpu.make_async_copy(
            pot_ref.at[:, pl.ds(b * tile, tile)], pot_in.at[b % 2], load_sem.at[b % 2]
        )
        for b in range(tiles)
    ]
    for b in range(min(2, tiles)):
        pot_copies[b].start()
    fit_copy.start()

    barrier = pltpu.get_barrier_semaphore()
    pl.semaphore_signal(barrier, inc=1, device_id={"grid": sib, "pts": p}, device_id_type=MESH)
    for r in range(1, chips):
        pl.semaphore_signal(
            barrier,
            inc=1,
            device_id={"grid": chip_at(r) * CORES + core, "pts": p},
            device_id_type=MESH,
        )
    for r in range(1, n_pts):
        pl.semaphore_signal(
            barrier, inc=1, device_id={"grid": g, "pts": pts_at(r)}, device_id_type=MESH
        )

    here = lax.broadcasted_iota(jnp.int32, (cap, cap), 0)
    there = lax.broadcasted_iota(jnp.int32, (cap, cap), 1)
    row_id = lax.broadcasted_iota(jnp.int32, (cap, rows_dev), 1).astype(F32)
    for q in range(n_pts):
        listed = rows_ref[0, q : q + 1, :]
        valid = there < count_ref[0:1, q : q + 1]
        wanted = jnp.where(valid, jnp.broadcast_to(listed, (cap, cap)), -1).astype(F32)
        column = jnp.sum(jnp.where(here == there, wanted, 0.0), axis=1, keepdims=True)
        pick = jnp.where(row_id == column, 1.0, 0.0).astype(BF16)
        piece[p, q] = jnp.dot(pick, orb_ref[...], preferred_element_type=F32).astype(BF16)
    pl.semaphore_wait(barrier, 1 + (chips - 1) + (n_pts - 1))

    a_copies = []
    for k in range(n_pts):
        for r in range(1, n_pts):
            q = (p + r + k) % n_pts
            copy = pltpu.make_async_remote_copy(
                src_ref=piece.at[p, q],
                dst_ref=piece.at[p, q],
                send_sem=a_send.at[r, k],
                recv_sem=a_recv.at[r, k],
                device_id={"grid": g, "pts": pts_at(r)},
                device_id_type=MESH,
            )
            copy.start()
            a_copies.append(copy)

    def a_wait(k):
        for r in range(1, n_pts):
            z, q = (p + n_pts - r) % n_pts, (p + k) % n_pts
            pltpu.make_async_remote_copy(
                src_ref=piece.at[z, q],
                dst_ref=piece.at[z, q],
                send_sem=a_send.at[r, k],
                recv_sem=a_recv.at[r, k],
                device_id={"grid": g, "pts": pts_at(r)},
                device_id_type=MESH,
            ).wait_recv()

    def gather_copy(buf, tag, r, to_sib):
        src = buf.at[rows_of(((chip + chips - r) % chips) * CORES + core)]
        return pltpu.make_async_remote_copy(
            src_ref=src,
            dst_ref=src,
            send_sem=s_send.at[tag, r],
            recv_sem=s_recv.at[tag, r],
            device_id={"grid": sib, "pts": p},
            device_id_type=MESH,
        )

    def gather_start(buf, tag):
        copies = []
        mine = buf.at[rows_of(g)]
        for r in range(1, chips):
            copies.append(
                pltpu.make_async_remote_copy(
                    src_ref=mine,
                    dst_ref=mine,
                    send_sem=c_send.at[tag, r],
                    recv_sem=c_recv.at[tag, r],
                    device_id={"grid": chip_at(r) * CORES + core, "pts": p},
                    device_id_type=MESH,
                )
            )
        copies.append(gather_copy(buf, tag, 0, True))
        for copy in copies:
            copy.start()
        return copies

    def gather_finish(buf, tag):
        copies = []
        for r in range(1, chips):
            came = buf.at[rows_of(((chip + chips - r) % chips) * CORES + core)]
            pltpu.make_async_remote_copy(
                src_ref=came,
                dst_ref=came,
                send_sem=c_send.at[tag, r],
                recv_sem=c_recv.at[tag, r],
                device_id={"grid": chip_at(r) * CORES + core, "pts": p},
                device_id_type=MESH,
            ).wait_recv()
            copy = gather_copy(buf, tag, r, True)
            copy.start()
            copies.append(copy)
        for r in range(chips):
            came = buf.at[rows_of(((chip + chips - r) % chips) * CORES + (1 - core))]
            pltpu.make_async_remote_copy(
                src_ref=came,
                dst_ref=came,
                send_sem=s_send.at[tag, r],
                recv_sem=s_recv.at[tag, r],
                device_id={"grid": sib, "pts": p},
                device_id_type=MESH,
            ).wait_recv()
        return copies

    pending = list(a_copies)
    a_wait(0)
    own[rows_of(g), :] = jnp.concatenate(
        [piece[z, p].astype(F32) for z in range(n_pts)], axis=0
    ).astype(BF16)
    pending += gather_start(own, 0)

    for b in range(tiles):
        pot_copies[b].wait()
        pot[b * tile : (b + 1) * tile, :] = pot_in[b % 2].astype(F32).T.astype(BF16)
        if b + 2 < tiles:
            pot_copies[b + 2].start()

    pending += gather_finish(own, 0)
    for k in range(1, n_pts):
        a_wait(k)
    for q in range(n_pts):
        cols[q * block : (q + 1) * block, :] = jnp.concatenate(
            [piece[z, q].astype(F32) for z in range(n_pts)], axis=0
        ).astype(BF16)

    def term(b, carry):
        rows = pl.ds(pl.multiple_of(b * tile, tile), tile)
        pair = lax.dot_general(
            own[rows, :], cols[...], (((1,), (1,)), ((), ())), preferred_element_type=F32
        )
        weighted = (pot[rows, :].astype(F32) * pair).astype(BF16)
        part[rows, :] = jnp.dot(weighted, cols[...], preferred_element_type=F32)
        return carry

    lax.fori_loop(0, tiles, term, 0)

    def bands(h):
        return slice(h * half, (h + 1) * half)

    def sib_copy(h):
        return pltpu.make_async_remote_copy(
            src_ref=sib_out.at[h],
            dst_ref=sib_in.at[h],
            send_sem=d_send.at[h],
            recv_sem=d_recv.at[h],
            device_id={"grid": sib, "pts": p},
            device_id_type=MESH,
        )

    def chip_copy(h, r):
        return pltpu.make_async_remote_copy(
            src_ref=chip_out.at[h, r],
            dst_ref=chip_in.at[h, r],
            send_sem=e_send.at[h, r],
            recv_sem=e_recv.at[h, r],
            device_id={"grid": chip_at(r) * CORES + core, "pts": p},
            device_id_type=MESH,
        )

    for h in range(HALVES):
        for k in range(chips):
            sib_out[h, k] = part[rows_of(k * CORES + (1 - core)), bands(h)].astype(BF16)
        copy = sib_copy(h)
        copy.start()
        pending.append(copy)
    for h in range(HALVES):
        sib_copy(h).wait_recv()
        for r in range(1, chips):
            k = chip_at(r)
            chip_out[h, r] = (
                part[rows_of(k * CORES + core), bands(h)] + sib_in[h, k].astype(F32)
            ).astype(BF16)
            copy = chip_copy(h, r)
            copy.start()
            pending.append(copy)
    for h in range(HALVES):
        total = part[rows_of(g), bands(h)] + sib_in[h, chip].astype(F32)
        for r in range(1, chips):
            chip_copy(h, r).wait_recv()
            total = total + chip_in[h, r].astype(F32)
        proj[h, rows_of(g), :] = total.astype(BF16)
        pending += gather_start(proj.at[h], 1 + h)

    def up_copy(h, j):
        return pltpu.make_async_remote_copy(
            src_ref=z_out.at[h, j],
            dst_ref=z_in.at[h, j + 1],
            send_sem=up_send.at[h, j],
            recv_sem=up_recv.at[h, j],
            device_id={"grid": g, "pts": jnp.minimum(p + 1, n_pts - 1)},
            device_id_type=MESH,
        )

    def dn_copy(h, j):
        return pltpu.make_async_remote_copy(
            src_ref=z_out.at[h, j],
            dst_ref=z_in.at[h, j],
            send_sem=dn_send.at[h, j],
            recv_sem=dn_recv.at[h, j],
            device_id={"grid": g, "pts": jnp.maximum(p - 1, 0)},
            device_id_type=MESH,
        )

    order = []
    for s in range(n_pts // 2):
        order += [n_pts - 1 - s, s]
    order += [j for j in range(n_pts) if j not in order]
    fit_copy.wait()
    for h in range(HALVES):
        pending += gather_finish(proj.at[h], 1 + h)
        for j in order:
            exch[h, j] = jnp.dot(
                fit[j * rows_dev : (j + 1) * rows_dev, :], proj[h], preferred_element_type=F32
            )
            if j > 0:

                @pl.when(p == 0)
                def _(h=h, j=j):
                    z_out[h, j] = exch[h, j].astype(BF16)
                    up_copy(h, j).start()

            if j < n_pts - 1:

                @pl.when(p == n_pts - 1)
                def _(h=h, j=j):
                    z_out[h, j] = exch[h, j].astype(BF16)
                    dn_copy(h, j).start()

    for h in range(HALVES):
        for s in range(n_pts - 1):
            up_j, dn_j = n_pts - 1 - s, s

            @pl.when((p > 0) & (p < up_j))
            def _(h=h, j=up_j):
                up_copy(h, j).wait_recv()
                z_out[h, j] = (exch[h, j] + z_in[h, j + 1].astype(F32)).astype(BF16)
                up_copy(h, j).start()

            @pl.when((p < n_pts - 1) & (p > dn_j))
            def _(h=h, j=dn_j):
                dn_copy(h, j).wait_recv()
                z_out[h, j] = (exch[h, j] + z_in[h, j].astype(F32)).astype(BF16)
                dn_copy(h, j).start()

    for h in range(HALVES):
        prj_ref[:, bands(h)] = proj[h]
    for h in range(HALVES):

        @pl.when(p > 0)
        def _(h=h):
            up_copy(h, p).wait_recv()
            exch[h, p] = exch[h, p] + z_in[h, p + 1].astype(F32)

        @pl.when(p < n_pts - 1)
        def _(h=h):
            dn_copy(h, p).wait_recv()
            exch[h, p] = exch[h, p] + z_in[h, p].astype(F32)

        upd_ref[:, bands(h)] = (orb_ref[:, bands(h)].astype(F32) - exch[h, p]).astype(BF16)

    for copy in pending:
        copy.wait_send()
    for h in range(HALVES):
        for j in range(n_pts):

            @pl.when(p < j)
            def _(h=h, j=j):
                up_copy(h, j).wait_send()

            @pl.when(p > j)
            def _(h=h, j=j):
                dn_copy(h, j).wait_send()


def on_device(n_grid, n_pts, orbitals, point_rows, point_count, potential, fitted_basis):
    rows_dev, width = orbitals.shape
    cap = point_rows.shape[2]
    block = n_pts * cap
    own_count = n_grid * block
    col_count = n_pts * block
    chips = n_grid // CORES
    half = width // HALVES
    tile = next(t for t in (256, 128, own_count) if own_count % t == 0)
    tags = 1 + HALVES
    pot_cols = jnp.transpose(potential, (1, 2, 0)).reshape(col_count, own_count)
    dma = pltpu.SemaphoreType.DMA
    buffers = [
        (fitted_basis.shape, BF16),
        ((2, col_count, tile), BF16),
        ((own_count, col_count), BF16),
        ((n_pts, n_pts, cap, width), BF16),
        ((col_count, width), BF16),
        ((own_count, width), BF16),
        ((own_count, width), F32),
        ((HALVES, chips, block, half), BF16),
        ((HALVES, chips, block, half), BF16),
        ((HALVES, chips, block, half), BF16),
        ((HALVES, chips, block, half), BF16),
        ((HALVES, own_count, half), BF16),
        ((HALVES, n_pts, rows_dev, half), F32),
        ((HALVES, n_pts, rows_dev, half), BF16),
        ((HALVES, n_pts + 1, rows_dev, half), BF16),
    ]
    used = 0
    for shape, dtype in buffers:
        size = jnp.dtype(dtype).itemsize
        for extent in shape:
            size *= extent
        used += size
    flops = 4 * own_count * col_count * width + 2 * fitted_basis.size * width
    vmem = pl.BlockSpec(memory_space=pltpu.VMEM)
    hbm = pl.BlockSpec(memory_space=pl.ANY)
    return pl.pallas_call(
        functools.partial(kernel, n_grid, n_pts, tile),
        out_shape=(
            jax.ShapeDtypeStruct((rows_dev, width), BF16),
            jax.ShapeDtypeStruct((own_count, width), BF16),
        ),
        in_specs=[vmem, vmem, vmem, hbm, hbm],
        out_specs=(vmem, vmem),
        scratch_shapes=[pltpu.VMEM(shape, dtype) for shape, dtype in buffers]
        + [
            dma((3,)),
            dma((n_pts, n_pts)),
            dma((n_pts, n_pts)),
            dma((tags, chips)),
            dma((tags, chips)),
            dma((tags, chips)),
            dma((tags, chips)),
            dma((HALVES,)),
            dma((HALVES,)),
            dma((HALVES, chips)),
            dma((HALVES, chips)),
            dma((HALVES, n_pts)),
            dma((HALVES, n_pts)),
            dma((HALVES, n_pts)),
            dma((HALVES, n_pts)),
        ],
        compiler_params=pltpu.CompilerParams(
            collective_id=0,
            has_side_effects=True,
            vmem_limit_bytes=min(used + used // 8 + (8 << 20), 62 << 20),
        ),
        cost_estimate=pl.CostEstimate(
            flops=flops, bytes_accessed=2 * (fitted_basis.size + potential.size), transcendentals=0
        ),
    )(orbitals, point_rows, point_count, pot_cols, fitted_basis)


def solution(mesh):
    in_specs = (
        P(("grid", "pts"), None),
        P(("grid", "pts"), None, None),
        P(("grid", "pts"), None),
        P("pts", None, "grid"),
        P("grid", "pts"),
    )
    out_specs = (P(("grid", "pts"), None), P("pts", None))
    return jax.shard_map(
        functools.partial(on_device, mesh.shape["grid"], mesh.shape["pts"]),
        mesh=mesh,
        in_specs=in_specs,
        out_specs=out_specs,
        check_vma=False,
    )
```

time: 154 us -> 67.4 us (0.44)
  waiting for transfers between devices: 79 us -> 0 us
  Pallas kernels: 0 us -> 60.2 us
  blocking collectives: 48 us -> 0 us
  between operations: 14.1 us -> 0.65 us
  matrix products: 4.51 us -> 0 us
  other arithmetic: 3.75 us -> 0 us
  local copies, waits for them, and re-layouts: 4.65 us -> 6.33 us
    reduce_scatter x2 -> x0, waiting for transfers between devices: 78.9 us -> none  [the longest x1 43 us: on_device(): lax.psum_scatter(jnp.dot(fitted_basis, projection, preferred_element_type...]
    pallas_call x0 -> x1, Pallas kernels: none -> 60.2 us  [on_device(): pl.pallas_call(functools.partial(kernel, n_grid, n_pts, tile), out_shape=...]
    all_gather x3 -> x0, blocking collectives: 36 us -> none  [the longest x1 15.3 us: on_device(): piece = lax.all_gather(slot_rows, 'pts', axis=0, tiled=True)]
    all_to_all x1 -> x0, blocking collectives: 12 us -> none  [on_device(): lax.all_to_all(picked, 'pts', split_axis=0, concat_axis=0, tiled=True)]
    dot_general x2 -> x0, matrix products: 4.51 us -> none  [the longest x1 2.36 us: on_device(): jnp.dot(fitted_basis, projection, preferred_element_type=jnp.float32)]
    unnamed x9 -> x12, local copies, waits for them, and re-layouts: 2.79 us -> 6.33 us
    convert_element_type x2 -> x0, other arithmetic: 2.04 us -> none  [the longest x1 1.1 us: on_device(): updated = (orbitals.astype(jnp.float32) - exchange).astype(jnp.bfloat16)]
    gather x1 -> x0, local copies, waits for them, and re-layouts: 1.78 us -> none  [on_device(): picked = jnp.take(orbitals, point_rows[0], axis=0)]
  transfers between devices with their start and end apart: 2 -> 0, of which waited for: 2 -> 0; matrix products, arithmetic and copies ran while one was open for 0% -> 0% of each run, Pallas kernels for 0% -> 0%
where the time goes in v1:
time: 67.4 us; the launch traced here: 67.2 us
  Pallas kernels  60.2 us (89%)
  local copies, waits for them, and re-layouts  6.33 us (9%)
    pallas_call x1, Pallas kernels, on_device(): pl.pallas_call(functools.partial(kernel, n_grid, n_pts, tile), out_shape=...  60.2 us
    unnamed x12, local copies, waits for them, and re-layouts  6.33 us

profile of v1, /device:TPU:0, one launch (start us, length us, event | category | flops | bytes accessed | tf_op | source)
XLA Modules:
  0.0 67.2 jit_solution(5985175555130231590)
XLA Ops:
  0.6 0.0 copy-start
  0.6 1.4 %copy-done = bf16[1024,768]{1,0:T(8,128)(2,1)S(1)} copy-done((bf16[1024,768]{1,0:T(8,128)(2,1)S(1)}, bf16[1024,768]{1,0:T(8,128)(2,1)}, u32[]{:S(2)}) %copy-start) | copy-done | bytes 1572888
  2.0 0.0 copy-start.1
  2.0 1.1 %copy-done.1 = bf16[768,4,96]{0,2,1:T(8,128)(2,1)S(1)} copy-done((bf16[768,4,96]{0,2,1:T(8,128)(2,1)S(1)}, bf16[768,4,96]{0,2,1:T(8,128)(2,1)}, u32[]{:S(2)}) %copy-start.1) | copy-done | bytes 589848
  3.1 0.0 copy-start.2
  3.1 0.9 %copy-done.2 = bf16[256,512]{1,0:T(8,128)(2,1)S(1)} copy-done((bf16[256,512]{1,0:T(8,128)(2,1)S(1)}, bf16[256,512]{1,0:T(8,128)(2,1)}, u32[]{:S(2)}) %copy-start.2) | copy-done | bytes 262168
  4.1 0.0 copy-start.3
  4.1 0.7 %copy-done.3 = s32[1,4,24]{2,1,0:T(4,128)S(1)} copy-done((s32[1,4,24]{2,1,0:T(4,128)S(1)}, s32[1,4,24]{2,1,0:T(4,128)}, u32[]{:S(2)}) %copy-start.3) | copy-done | bytes 408
  4.7 0.0 copy-start.4
  4.7 0.7 copy-done.4
  5.4 60.2 %shard_map.68 = (bf16[256,512]{1,0:T(8,128)(2,1)S(1)}, bf16[768,512]{1,0:T(8,128)(2,1)S(1)}) custom-call(bf16[256,512]{1,0:T(8,128)(2,1)S(1)} %copy-done.2, s32[1,4,24]{2,1,0:T(4,128)S(1)} %copy-done.3, s32[1,4]{1,0:T(1,128)S(1)} %copy-done.4, bf16[384,768]{1,0:T(8,128)(2,1)S(1)} %bitcast.3, bf16[1024,768]{1,0:T(8,128)(2,1)S(1)} %copy-done), custom_call_target="tpu_custom_call" | custom-call | flops 1409286144 | bytes 2162688 | tf_op jit(solution)/shard_map/pallas_call | solution.py:409
  65.6 0.7 %copy.9 = bf16[256,512]{1,0:T(8,128)(2,1)} copy(bf16[256,512]{1,0:T(8,128)(2,1)S(1)} %get-tuple-element.4) | data formatting | bytes 524288
  66.3 0.9 %copy.10 = bf16[768,512]{1,0:T(8,128)(2,1)} copy(bf16[768,512]{1,0:T(8,128)(2,1)S(1)} %get-tuple-element.5) | data formatting | bytes 1572864
Async XLA Ops:
  0.6 1.4 %copy-start = (bf16[1024,768]{1,0:T(8,128)(2,1)S(1)}, bf16[1024,768]{1,0:T(8,128)(2,1)}, u32[]{:S(2)}) copy-start(bf16[1024,768]{1,0:T(8,128)(2,1)} %fit_ref.1) | copy-start | bytes 4718596
  2.0 1.1 %copy-start.1 = (bf16[768,4,96]{0,2,1:T(8,128)(2,1)S(1)}, bf16[768,4,96]{0,2,1:T(8,128)(2,1)}, u32[]{:S(2)}) copy-start(bf16[768,4,96]{0,2,1:T(8,128)(2,1)} %param.8) | copy-start | bytes 1769476
  3.1 0.9 %copy-start.2 = (bf16[256,512]{1,0:T(8,128)(2,1)S(1)}, bf16[256,512]{1,0:T(8,128)(2,1)}, u32[]{:S(2)}) copy-start(bf16[256,512]{1,0:T(8,128)(2,1)} %orb_ref.1) | copy-start | bytes 786436
  4.1 0.7 %copy-start.3 = (s32[1,4,24]{2,1,0:T(4,128)S(1)}, s32[1,4,24]{2,1,0:T(4,128)}, u32[]{:S(2)}) copy-start(s32[1,4,24]{2,1,0:T(4,128)} %rows_ref.1) | copy-start | bytes 1156
  4.7 0.7 copy-start.4

commit v2 on v1

--- a/solution.py
+++ b/solution.py
@@ -11,6 +11,7 @@
 F32 = jnp.float32
 BF16 = jnp.bfloat16
 CORES = 2
+VMEM_BYTES = 63 << 20
 HALVES = 2
 
 
@@ -18,14 +19,20 @@
     n_grid,
     n_pts,
     tile,
+    orb_hbm,
+    rows_hbm,
+    count_hbm,
+    pot_ref,
+    fit_ref,
+    upd_hbm,
+    prj_hbm,
     orb_ref,
     rows_ref,
     count_ref,
-    pot_ref,
-    fit_ref,
     upd_ref,
-    prj_ref,
     fit,
+    fit_far,
+    proj_far,
     pot_in,
     pot,
     piece,
@@ -55,6 +62,9 @@
     up_recv,
     dn_send,
     dn_recv,
+    far_send,
+    far_recv,
+    out_sem,
 ):
     g = lax.axis_index("grid")
     p = lax.axis_index("pts")
@@ -77,6 +87,14 @@
     def rows_of(gg):
         return pl.ds(pl.multiple_of(gg * block, block), block)
 
+    first_copies = [
+        pltpu.make_async_copy(src, dst, load_sem.at[3 + i])
+        for i, (src, dst) in enumerate(
+            ((rows_hbm, rows_ref), (count_hbm, count_ref), (orb_hbm, orb_ref))
+        )
+    ]
+    for copy in first_copies:
+        copy.start()
     fit_copy = pltpu.make_async_copy(fit_ref, fit, load_sem.at[2])
     pot_copies = [
         pltpu.make_async_copy(
@@ -84,9 +102,6 @@
         )
         for b in range(tiles)
     ]
-    for b in range(min(2, tiles)):
-        pot_copies[b].start()
-    fit_copy.start()
 
     barrier = pltpu.get_barrier_semaphore()
     pl.semaphore_signal(barrier, inc=1, device_id={"grid": sib, "pts": p}, device_id_type=MESH)
@@ -102,8 +117,14 @@
             barrier, inc=1, device_id={"grid": g, "pts": pts_at(r)}, device_id_type=MESH
         )
 
+    for b in range(min(2, tiles)):
+        pot_copies[b].start()
+    fit_copy.start()
+
     here = lax.broadcasted_iota(jnp.int32, (cap, cap), 0)
     there = lax.broadcasted_iota(jnp.int32, (cap, cap), 1)
+    for copy in first_copies:
+        copy.wait()
     row_id = lax.broadcasted_iota(jnp.int32, (cap, rows_dev), 1).astype(F32)
     for q in range(n_pts):
         listed = rows_ref[0, q : q + 1, :]
@@ -141,7 +162,33 @@
                 device_id_type=MESH,
             ).wait_recv()
 
-    def gather_copy(buf, tag, r, to_sib):
+    far = n_pts >= 4
+    first_up, last_dn = (2, n_pts - 3) if far else (1, n_pts - 2)
+    at_end = (p == 0) | (p == n_pts - 1)
+    at_near = (p == 1) | (p == n_pts - 2)
+    inner = 1 + (p * max(n_pts - 3, 0)) // max(n_pts - 1, 1)
+
+    def far_fit_copy():
+        return pltpu.make_async_remote_copy(
+            src_ref=fit.at[pl.ds(pl.multiple_of(inner * rows_dev, rows_dev), rows_dev)],
+            dst_ref=fit_far,
+            send_sem=far_send.at[0],
+            recv_sem=far_recv.at[0],
+            device_id={"grid": g, "pts": inner},
+            device_id_type=MESH,
+        )
+
+    def far_share_copy(h):
+        return pltpu.make_async_remote_copy(
+            src_ref=proj.at[h, rows_of(g)],
+            dst_ref=proj_far.at[h, rows_of(g)],
+            send_sem=far_send.at[1 + h],
+            recv_sem=far_recv.at[1 + h],
+            device_id={"grid": g, "pts": inner},
+            device_id_type=MESH,
+        )
+
+    def gather_copy(buf, tag, r):
         src = buf.at[rows_of(((chip + chips - r) % chips) * CORES + core)]
         return pltpu.make_async_remote_copy(
             src_ref=src,
@@ -152,21 +199,20 @@
             device_id_type=MESH,
         )
 
+    def gather_chip(buf, tag, r, gg):
+        src = buf.at[rows_of(gg)]
+        return pltpu.make_async_remote_copy(
+            src_ref=src,
+            dst_ref=src,
+            send_sem=c_send.at[tag, r],
+            recv_sem=c_recv.at[tag, r],
+            device_id={"grid": chip_at(r) * CORES + core, "pts": p},
+            device_id_type=MESH,
+        )
+
     def gather_start(buf, tag):
-        copies = []
-        mine = buf.at[rows_of(g)]
-        for r in range(1, chips):
-            copies.append(
-                pltpu.make_async_remote_copy(
-                    src_ref=mine,
-                    dst_ref=mine,
-                    send_sem=c_send.at[tag, r],
-                    recv_sem=c_recv.at[tag, r],
-                    device_id={"grid": chip_at(r) * CORES + core, "pts": p},
-                    device_id_type=MESH,
-                )
-            )
-        copies.append(gather_copy(buf, tag, 0, True))
+        copies = [gather_chip(buf, tag, r, g) for r in range(1, chips)]
+        copies.append(gather_copy(buf, tag, 0))
         for copy in copies:
             copy.start()
         return copies
@@ -174,16 +220,9 @@
     def gather_finish(buf, tag):
         copies = []
         for r in range(1, chips):
-            came = buf.at[rows_of(((chip + chips - r) % chips) * CORES + core)]
-            pltpu.make_async_remote_copy(
-                src_ref=came,
-                dst_ref=came,
-                send_sem=c_send.at[tag, r],
-                recv_sem=c_recv.at[tag, r],
-                device_id={"grid": chip_at(r) * CORES + core, "pts": p},
-                device_id_type=MESH,
-            ).wait_recv()
-            copy = gather_copy(buf, tag, r, True)
+            gg = ((chip + chips - r) % chips) * CORES + core
+            gather_chip(buf, tag, r, gg).wait_recv()
+            copy = gather_copy(buf, tag, r)
             copy.start()
             copies.append(copy)
         for r in range(chips):
@@ -214,6 +253,19 @@
     pending += gather_finish(own, 0)
     for k in range(1, n_pts):
         a_wait(k)
+    if far:
+
+        @pl.when(at_end)
+        def _():
+            fit_copy.wait()
+            far_fit_copy().start()
+
+        @pl.when(jnp.logical_not(at_end))
+        def _():
+            fit_copy.wait()
+
+    else:
+        fit_copy.wait()
     for q in range(n_pts):
         cols[q * block : (q + 1) * block, :] = jnp.concatenate(
             [piece[z, q].astype(F32) for z in range(n_pts)], axis=0
@@ -224,8 +276,7 @@
         pair = lax.dot_general(
             own[rows, :], cols[...], (((1,), (1,)), ((), ())), preferred_element_type=F32
         )
-        weighted = (pot[rows, :].astype(F32) * pair).astype(BF16)
-        part[rows, :] = jnp.dot(weighted, cols[...], preferred_element_type=F32)
+        pot[rows, :] = (pot[rows, :].astype(F32) * pair).astype(BF16)
         return carry
 
     lax.fori_loop(0, tiles, term, 0)
@@ -254,6 +305,15 @@
         )
 
     for h in range(HALVES):
+
+        def product(b, carry, h=h):
+            rows = pl.ds(pl.multiple_of(b * tile, tile), tile)
+            part[rows, bands(h)] = jnp.dot(
+                pot[rows, :], cols[:, bands(h)], preferred_element_type=F32
+            )
+            return carry
+
+        lax.fori_loop(0, tiles, product, 0)
         for k in range(chips):
             sib_out[h, k] = part[rows_of(k * CORES + (1 - core)), bands(h)].astype(BF16)
         copy = sib_copy(h)
@@ -276,6 +336,26 @@
             total = total + chip_in[h, r].astype(F32)
         proj[h, rows_of(g), :] = total.astype(BF16)
         pending += gather_start(proj.at[h], 1 + h)
+        if far:
+
+            @pl.when(at_end)
+            def _(h=h):
+                far_share_copy(h).start()
+
+    def far_start(h):
+        if far:
+
+            @pl.when(at_near)
+            def _():
+                far_share_copy(h).wait_recv()
+                gather_start(proj_far.at[h], 1 + HALVES + h)
+
+    def far_finish(h):
+        if far:
+
+            @pl.when(at_near)
+            def _():
+                gather_finish(proj_far.at[h], 1 + HALVES + h)
 
     def up_copy(h, j):
         return pltpu.make_async_remote_copy(
@@ -301,29 +381,35 @@
     for s in range(n_pts // 2):
         order += [n_pts - 1 - s, s]
     order += [j for j in range(n_pts) if j not in order]
-    fit_copy.wait()
     for h in range(HALVES):
         pending += gather_finish(proj.at[h], 1 + h)
         for j in order:
             exch[h, j] = jnp.dot(
                 fit[j * rows_dev : (j + 1) * rows_dev, :], proj[h], preferred_element_type=F32
             )
-            if j > 0:
+            if j >= first_up:
 
                 @pl.when(p == 0)
                 def _(h=h, j=j):
                     z_out[h, j] = exch[h, j].astype(BF16)
                     up_copy(h, j).start()
 
-            if j < n_pts - 1:
+            if j <= last_dn:
 
                 @pl.when(p == n_pts - 1)
                 def _(h=h, j=j):
                     z_out[h, j] = exch[h, j].astype(BF16)
                     dn_copy(h, j).start()
 
-    for h in range(HALVES):
-        for s in range(n_pts - 1):
+        far_start(h)
+
+    prj_copies = []
+    for h in range(HALVES):
+        copy = pltpu.make_async_copy(proj.at[h], prj_hbm.at[:, bands(h)], out_sem.at[h])
+        copy.start()
+        prj_copies.append(copy)
+    for h in range(HALVES):
+        for s in range(n_pts - first_up):
             up_j, dn_j = n_pts - 1 - s, s
 
             @pl.when((p > 0) & (p < up_j))
@@ -338,34 +424,72 @@
                 z_out[h, j] = (exch[h, j] + z_in[h, j].astype(F32)).astype(BF16)
                 dn_copy(h, j).start()
 
-    for h in range(HALVES):
-        prj_ref[:, bands(h)] = proj[h]
-    for h in range(HALVES):
-
-        @pl.when(p > 0)
+        far_finish(h)
+
+    upd_copies = []
+    for h in range(HALVES):
+        if far:
+
+            @pl.when(at_near)
+            def _(h=h):
+                if h == 0:
+                    far_fit_copy().wait_recv()
+                exch[h, p] = exch[h, p] + jnp.dot(
+                    fit_far[...], proj_far[h], preferred_element_type=F32
+                )
+
+        @pl.when(p >= first_up)
         def _(h=h):
             up_copy(h, p).wait_recv()
             exch[h, p] = exch[h, p] + z_in[h, p + 1].astype(F32)
 
-        @pl.when(p < n_pts - 1)
+        @pl.when(p <= last_dn)
         def _(h=h):
             dn_copy(h, p).wait_recv()
             exch[h, p] = exch[h, p] + z_in[h, p].astype(F32)
 
         upd_ref[:, bands(h)] = (orb_ref[:, bands(h)].astype(F32) - exch[h, p]).astype(BF16)
-
+        copy = pltpu.make_async_copy(
+            upd_ref.at[:, bands(h)], upd_hbm.at[:, bands(h)], out_sem.at[HALVES + h]
+        )
+        copy.start()
+        upd_copies.append(copy)
+
+    if far:
+
+        @pl.when(at_end)
+        def _():
+            far_fit_copy().wait_send()
+            for h in range(HALVES):
+                far_share_copy(h).wait_send()
+
+        @pl.when(at_near)
+        def _():
+            for h in range(HALVES):
+                tag = 1 + HALVES + h
+                for r in range(chips):
+                    gather_copy(proj_far.at[h], tag, r).wait_send()
+                    if r > 0:
+                        gather_chip(proj_far.at[h], tag, r, g).wait_send()
+
+    for copy in prj_copies + upd_copies:
+        copy.wait()
     for copy in pending:
         copy.wait_send()
     for h in range(HALVES):
         for j in range(n_pts):
 
-            @pl.when(p < j)
-            def _(h=h, j=j):
-                up_copy(h, j).wait_send()
-
-            @pl.when(p > j)
-            def _(h=h, j=j):
-                dn_copy(h, j).wait_send()
+            if j >= first_up:
+
+                @pl.when(p < j)
+                def _(h=h, j=j):
+                    up_copy(h, j).wait_send()
+
+            if j <= last_dn:
+
+                @pl.when(p > j)
+                def _(h=h, j=j):
+                    dn_copy(h, j).wait_send()
 
 
 def on_device(n_grid, n_pts, orbitals, point_rows, point_count, potential, fitted_basis):
@@ -377,11 +501,17 @@
     chips = n_grid // CORES
     half = width // HALVES
     tile = next(t for t in (256, 128, own_count) if own_count % t == 0)
-    tags = 1 + HALVES
+    tags = 1 + 2 * HALVES
     pot_cols = jnp.transpose(potential, (1, 2, 0)).reshape(col_count, own_count)
     dma = pltpu.SemaphoreType.DMA
     buffers = [
+        ((rows_dev, width), BF16),
+        (point_rows.shape, jnp.int32),
+        (point_count.shape, jnp.int32),
+        ((rows_dev, width), BF16),
         (fitted_basis.shape, BF16),
+        ((rows_dev, own_count), BF16),
+        ((HALVES, own_count, half), BF16),
         ((2, col_count, tile), BF16),
         ((own_count, col_count), BF16),
         ((n_pts, n_pts, cap, width), BF16),
@@ -397,14 +527,7 @@
         ((HALVES, n_pts, rows_dev, half), BF16),
         ((HALVES, n_pts + 1, rows_dev, half), BF16),
     ]
-    used = 0
-    for shape, dtype in buffers:
-        size = jnp.dtype(dtype).itemsize
-        for extent in shape:
-            size *= extent
-        used += size
     flops = 4 * own_count * col_count * width + 2 * fitted_basis.size * width
-    vmem = pl.BlockSpec(memory_space=pltpu.VMEM)
     hbm = pl.BlockSpec(memory_space=pl.ANY)
     return pl.pallas_call(
         functools.partial(kernel, n_grid, n_pts, tile),
@@ -412,11 +535,11 @@
             jax.ShapeDtypeStruct((rows_dev, width), BF16),
             jax.ShapeDtypeStruct((own_count, width), BF16),
         ),
-        in_specs=[vmem, vmem, vmem, hbm, hbm],
-        out_specs=(vmem, vmem),
+        in_specs=[hbm] * 5,
+        out_specs=(hbm, hbm),
         scratch_shapes=[pltpu.VMEM(shape, dtype) for shape, dtype in buffers]
         + [
-            dma((3,)),
+            dma((6,)),
             dma((n_pts, n_pts)),
             dma((n_pts, n_pts)),
             dma((tags, chips)),
@@ -431,11 +554,14 @@
             dma((HALVES, n_pts)),
             dma((HALVES, n_pts)),
             dma((HALVES, n_pts)),
+            dma((1 + HALVES,)),
+            dma((1 + HALVES,)),
+            dma((2 * HALVES,)),
         ],
         compiler_params=pltpu.CompilerParams(
             collective_id=0,
             has_side_effects=True,
-            vmem_limit_bytes=min(used + used // 8 + (8 << 20), 62 << 20),
+            vmem_limit_bytes=VMEM_BYTES,
         ),
         cost_estimate=pl.CostEstimate(
             flops=flops, bytes_accessed=2 * (fitted_basis.size + potential.size), transcendentals=0

time: 67.4 us -> 68.2 us (1.012)
  Pallas kernels: 60.2 us -> 63.6 us
  local copies, waits for them, and re-layouts: 6.33 us -> 3.73 us
    pallas_call x1, Pallas kernels: 60.2 us -> 63.6 us  [on_device(): pl.pallas_call(functools.partial(kernel, n_grid, n_pts, tile), out_shape=...]
    unnamed x12 -> x2, local copies, waits for them, and re-layouts: 6.33 us -> 3.73 us
where the time goes in v2:
time: 68.2 us; the launch traced here: 68 us
  Pallas kernels  63.6 us (93%)
  local copies, waits for them, and re-layouts  3.73 us (5%)
    pallas_call x1, Pallas kernels, on_device(): pl.pallas_call(functools.partial(kernel, n_grid, n_pts, tile), out_shape=...  63.6 us
    unnamed x2, local copies, waits for them, and re-layouts  3.73 us

profile of v2, /device:TPU:0, one launch (start us, length us, event | category | flops | bytes accessed | tf_op | source)
XLA Modules:
  0.0 68.0 jit_solution(13361360260022865529)
XLA Ops:
  0.6 63.6 %shard_map.68 = (bf16[256,512]{1,0:T(8,128)(2,1)}, bf16[768,512]{1,0:T(8,128)(2,1)}) custom-call(bf16[256,512]{1,0:T(8,128)(2,1)} %orb_hbm.1, s32[1,4,24]{2,1,0:T(4,128)} %rows_hbm.1, s32[1,4]{1,0:T(1,128)} %count_hbm.1, bf16[384,768]{1,0:T(8,128)(2,1)} %bitcast.3, bf16[1024,768]{1,0:T(8,128)(2,1)} %fit_ref.1), custom_call_target="tpu_custom_call" | custom-call | flops 1409286144 | bytes 2162688 | tf_op jit(solution)/shard_map/pallas_call | solution.py:532
  64.3 1.7 %copy.9 = bf16[256,512]{1,0:T(8,128)(2,1)} copy(bf16[256,512]{1,0:T(8,128)(2,1)} %get-tuple-element.4) | data formatting | bytes 524288
  65.9 2.1 %copy.10 = bf16[768,512]{1,0:T(8,128)(2,1)} copy(bf16[768,512]{1,0:T(8,128)(2,1)} %get-tuple-element.5) | data formatting | bytes 1572864

commit v3 on v2

--- a/solution.py
+++ b/solution.py
@@ -11,7 +11,9 @@
 F32 = jnp.float32
 BF16 = jnp.bfloat16
 CORES = 2
+FAR = False
 VMEM_BYTES = 63 << 20
+PIECES = 4
 HALVES = 2
 
 
@@ -162,7 +164,7 @@
                 device_id_type=MESH,
             ).wait_recv()
 
-    far = n_pts >= 4
+    far = FAR and n_pts >= 4
     first_up, last_dn = (2, n_pts - 3) if far else (1, n_pts - 2)
     at_end = (p == 0) | (p == n_pts - 1)
     at_near = (p == 1) | (p == n_pts - 2)
@@ -237,6 +239,15 @@
             ).wait_recv()
         return copies
 
+    def turn(b):
+        pot_copies[b].wait()
+        pot[b * tile : (b + 1) * tile, :] = pot_in[b % 2].astype(F32).T.astype(BF16)
+        if b + 2 < tiles:
+            pot_copies[b + 2].start()
+
+    early = (tiles + 1) // 2
+    for b in range(early):
+        turn(b)
     pending = list(a_copies)
     a_wait(0)
     own[rows_of(g), :] = jnp.concatenate(
@@ -244,12 +255,8 @@
     ).astype(BF16)
     pending += gather_start(own, 0)
 
-    for b in range(tiles):
-        pot_copies[b].wait()
-        pot[b * tile : (b + 1) * tile, :] = pot_in[b % 2].astype(F32).T.astype(BF16)
-        if b + 2 < tiles:
-            pot_copies[b + 2].start()
-
+    for b in range(early, tiles):
+        turn(b)
     pending += gather_finish(own, 0)
     for k in range(1, n_pts):
         a_wait(k)
@@ -403,30 +410,46 @@
 
         far_start(h)
 
-    prj_copies = []
+    out_copies = []
     for h in range(HALVES):
         copy = pltpu.make_async_copy(proj.at[h], prj_hbm.at[:, bands(h)], out_sem.at[h])
         copy.start()
-        prj_copies.append(copy)
-    for h in range(HALVES):
-        for s in range(n_pts - first_up):
-            up_j, dn_j = n_pts - 1 - s, s
-
-            @pl.when((p > 0) & (p < up_j))
-            def _(h=h, j=up_j):
-                up_copy(h, j).wait_recv()
-                z_out[h, j] = (exch[h, j] + z_in[h, j + 1].astype(F32)).astype(BF16)
-                up_copy(h, j).start()
-
-            @pl.when((p < n_pts - 1) & (p > dn_j))
-            def _(h=h, j=dn_j):
-                dn_copy(h, j).wait_recv()
-                z_out[h, j] = (exch[h, j] + z_in[h, j].astype(F32)).astype(BF16)
-                dn_copy(h, j).start()
+        out_copies.append(copy)
+    def relay_up(h, j):
+        @pl.when((p > 0) & (p < j))
+        def _():
+            up_copy(h, j).wait_recv()
+            z_out[h, j] = (exch[h, j] + z_in[h, j + 1].astype(F32)).astype(BF16)
+            up_copy(h, j).start()
+
+    def relay_dn(h, j):
+        @pl.when((p < n_pts - 1) & (p > j))
+        def _():
+            dn_copy(h, j).wait_recv()
+            z_out[h, j] = (exch[h, j] + z_in[h, j].astype(F32)).astype(BF16)
+            dn_copy(h, j).start()
+
+    lower = 2 * p < n_pts
+    ups = range(n_pts - 1, first_up - 1, -1)
+    dns = range(last_dn + 1)
+    for h in range(HALVES):
+
+        @pl.when(lower)
+        def _(h=h):
+            for j in ups:
+                relay_up(h, j)
+            for j in dns:
+                relay_dn(h, j)
+
+        @pl.when(jnp.logical_not(lower))
+        def _(h=h):
+            for j in dns:
+                relay_dn(h, j)
+            for j in ups:
+                relay_up(h, j)
 
         far_finish(h)
 
-    upd_copies = []
     for h in range(HALVES):
         if far:
 
@@ -453,7 +476,7 @@
             upd_ref.at[:, bands(h)], upd_hbm.at[:, bands(h)], out_sem.at[HALVES + h]
         )
         copy.start()
-        upd_copies.append(copy)
+        out_copies.append(copy)
 
     if far:
 
@@ -472,7 +495,7 @@
                     if r > 0:
                         gather_chip(proj_far.at[h], tag, r, g).wait_send()
 
-    for copy in prj_copies + upd_copies:
+    for copy in out_copies:
         copy.wait()
     for copy in pending:
         copy.wait_send()
@@ -490,6 +513,21 @@
                 @pl.when(p > j)
                 def _(h=h, j=j):
                     dn_copy(h, j).wait_send()
+
+
+def hand_over(upd_ref, prj_ref, upd_out, prj_out, sem):
+    copies = []
+    for i, (src, dst) in enumerate(((upd_ref, upd_out), (prj_ref, prj_out))):
+        rows = src.shape[0] // PIECES
+        for k in range(PIECES):
+            part = pl.ds(k * rows, rows)
+            copies.append(
+                pltpu.make_async_copy(src.at[part], dst.at[part], sem.at[i * PIECES + k])
+            )
+    for copy in copies:
+        copy.start()
+    for copy in copies:
+        copy.wait()
 
 
 def on_device(n_grid, n_pts, orbitals, point_rows, point_count, potential, fitted_basis):
@@ -529,7 +567,7 @@
     ]
     flops = 4 * own_count * col_count * width + 2 * fitted_basis.size * width
     hbm = pl.BlockSpec(memory_space=pl.ANY)
-    return pl.pallas_call(
+    updated, projection = pl.pallas_call(
         functools.partial(kernel, n_grid, n_pts, tile),
         out_shape=(
             jax.ShapeDtypeStruct((rows_dev, width), BF16),
@@ -567,6 +605,17 @@
             flops=flops, bytes_accessed=2 * (fitted_basis.size + potential.size), transcendentals=0
         ),
     )(orbitals, point_rows, point_count, pot_cols, fitted_basis)
+    return pl.pallas_call(
+        hand_over,
+        out_shape=(
+            jax.ShapeDtypeStruct(updated.shape, BF16),
+            jax.ShapeDtypeStruct(projection.shape, BF16),
+        ),
+        in_specs=[hbm] * 2,
+        out_specs=(hbm, hbm),
+        scratch_shapes=[dma((2 * PIECES,))],
+        compiler_params=pltpu.CompilerParams(vmem_limit_bytes=VMEM_BYTES),
+    )(updated, projection)
 
 
 def solution(mesh):

time: 68.2 us -> 89.7 us (1.32)
  Pallas kernels: 63.6 us -> 88.9 us
  local copies, waits for them, and re-layouts: 3.73 us -> 0 us
    pallas_call x0 -> x1, Pallas kernels: none -> 32.9 us  [on_device(): pl.pallas_call(hand_over, out_shape=(jax.ShapeDtypeStruct(updated.shape,...]
    pallas_call x1, Pallas kernels: 63.6 us -> 55.9 us  [on_device(): pl.pallas_call(functools.partial(kernel, n_grid, n_pts, tile), out_shape=...]
    unnamed x2 -> x0, local copies, waits for them, and re-layouts: 3.73 us -> none
where the time goes in v3:
time: 89.7 us; the launch traced here: 89.5 us
  Pallas kernels  88.9 us (99%)
    pallas_call x1, Pallas kernels, on_device(): pl.pallas_call(functools.partial(kernel, n_grid, n_pts, tile), out_shape=...  55.9 us
    pallas_call x1, Pallas kernels, on_device(): pl.pallas_call(hand_over, out_shape=(jax.ShapeDtypeStruct(updated.shape,...  32.9 us

profile of v3, /device:TPU:0, one launch (start us, length us, event | category | flops | bytes accessed | tf_op | source)
XLA Modules:
  0.0 89.5 jit_solution(8513160409734200953)
XLA Ops:
  0.6 55.9 %shard_map.68 = (bf16[256,512]{1,0:T(8,128)(2,1)}, bf16[768,512]{1,0:T(8,128)(2,1)}) custom-call(bf16[256,512]{1,0:T(8,128)(2,1)} %orb_hbm.1, s32[1,4,24]{2,1,0:T(4,128)} %rows_hbm.1, s32[1,4]{1,0:T(1,128)} %count_hbm.1, bf16[384,768]{1,0:T(8,128)(2,1)} %bitcast.3, bf16[1024,768]{1,0:T(8,128)(2,1)} %fit_ref.1), custom_call_target="tpu_custom_call" | custom-call | flops 1409286144 | bytes 2162688 | tf_op jit(solution)/shard_map/pallas_call | solution.py:570
  56.6 32.9 %shard_map.69 = (bf16[256,512]{1,0:T(8,128)(2,1)}, bf16[768,512]{1,0:T(8,128)(2,1)}) custom-call(bf16[256,512]{1,0:T(8,128)(2,1)} %get-tuple-element.4.upd_ref, bf16[768,512]{1,0:T(8,128)(2,1)} %get-tuple-element.5.prj_ref), custom_call_target="tpu_custom_call" | custom-call | tf_op jit(solution)/shard_map/pallas_call | solution.py:608

commit v4 on v3

--- a/solution.py
+++ b/solution.py
@@ -13,7 +13,7 @@
 CORES = 2
 FAR = False
 VMEM_BYTES = 63 << 20
-PIECES = 4
+PIECES = 2
 HALVES = 2
 
 
@@ -137,8 +137,8 @@
         piece[p, q] = jnp.dot(pick, orb_ref[...], preferred_element_type=F32).astype(BF16)
     pl.semaphore_wait(barrier, 1 + (chips - 1) + (n_pts - 1))
 
-    a_copies = []
-    for k in range(n_pts):
+    def a_start(k):
+        copies = []
         for r in range(1, n_pts):
             q = (p + r + k) % n_pts
             copy = pltpu.make_async_remote_copy(
@@ -150,7 +150,10 @@
                 device_id_type=MESH,
             )
             copy.start()
-            a_copies.append(copy)
+            copies.append(copy)
+        return copies
+
+    pending = a_start(0)
 
     def a_wait(k):
         for r in range(1, n_pts):
@@ -212,9 +215,13 @@
             device_id_type=MESH,
         )
 
-    def gather_start(buf, tag):
+    def gather_list(buf, tag):
         copies = [gather_chip(buf, tag, r, g) for r in range(1, chips)]
         copies.append(gather_copy(buf, tag, 0))
+        return copies
+
+    def gather_start(buf, tag):
+        copies = gather_list(buf, tag)
         for copy in copies:
             copy.start()
         return copies
@@ -248,12 +255,13 @@
     early = (tiles + 1) // 2
     for b in range(early):
         turn(b)
-    pending = list(a_copies)
     a_wait(0)
     own[rows_of(g), :] = jnp.concatenate(
         [piece[z, p].astype(F32) for z in range(n_pts)], axis=0
     ).astype(BF16)
     pending += gather_start(own, 0)
+    for k in range(1, n_pts):
+        pending += a_start(k)
 
     for b in range(early, tiles):
         turn(b)
@@ -326,6 +334,14 @@
         copy = sib_copy(h)
         copy.start()
         pending.append(copy)
+    def in_turn(copies, before):
+        for copy in before:
+            copy.wait_send()
+        for copy in copies:
+            copy.start()
+        return copies
+
+    sent = []
     for h in range(HALVES):
         sib_copy(h).wait_recv()
         for r in range(1, chips):
@@ -333,21 +349,23 @@
             chip_out[h, r] = (
                 part[rows_of(k * CORES + core), bands(h)] + sib_in[h, k].astype(F32)
             ).astype(BF16)
-            copy = chip_copy(h, r)
-            copy.start()
-            pending.append(copy)
+        sent = in_turn([chip_copy(h, r) for r in range(1, chips)], sent)
+    pending += sent
+    sent = []
     for h in range(HALVES):
         total = part[rows_of(g), bands(h)] + sib_in[h, chip].astype(F32)
         for r in range(1, chips):
             chip_copy(h, r).wait_recv()
             total = total + chip_in[h, r].astype(F32)
         proj[h, rows_of(g), :] = total.astype(BF16)
-        pending += gather_start(proj.at[h], 1 + h)
+        sent = in_turn(gather_list(proj.at[h], 1 + h), sent)
         if far:
 
             @pl.when(at_end)
             def _(h=h):
                 far_share_copy(h).start()
+
+    pending += sent
 
     def far_start(h):
         if far:
@@ -388,25 +406,40 @@
     for s in range(n_pts // 2):
         order += [n_pts - 1 - s, s]
     order += [j for j in range(n_pts) if j not in order]
+    def far_first(js):
+        return [(h, j) for h in range(HALVES) for j in js[:-1]] + [
+            (h, js[-1]) for h in range(HALVES)
+        ]
+
+    up_order = far_first(list(range(n_pts - 1, first_up - 1, -1)))
+    dn_order = far_first(list(range(last_dn + 1)))
+    lead_all = HALVES * (n_pts - 1 - first_up)
+
+    def end_send(copy_of, sequence, n):
+        h, j = sequence[n]
+        if n >= 2:
+            copy_of(*sequence[n - 2]).wait_send()
+        z_out[h, j] = exch[h, j].astype(BF16)
+        copy_of(h, j).start()
+
     for h in range(HALVES):
         pending += gather_finish(proj.at[h], 1 + h)
         for j in order:
             exch[h, j] = jnp.dot(
                 fit[j * rows_dev : (j + 1) * rows_dev, :], proj[h], preferred_element_type=F32
             )
-            if j >= first_up:
-
-                @pl.when(p == 0)
-                def _(h=h, j=j):
-                    z_out[h, j] = exch[h, j].astype(BF16)
-                    up_copy(h, j).start()
-
-            if j <= last_dn:
-
-                @pl.when(p == n_pts - 1)
-                def _(h=h, j=j):
-                    z_out[h, j] = exch[h, j].astype(BF16)
-                    dn_copy(h, j).start()
+
+        @pl.when(p == 0)
+        def _(h=h, last=h == HALVES - 1):
+            for n in range(len(up_order)):
+                if (up_order[n][0] == h and n < lead_all) or (last and n >= lead_all):
+                    end_send(up_copy, up_order, n)
+
+        @pl.when(p == n_pts - 1)
+        def _(h=h, last=h == HALVES - 1):
+            for n in range(len(dn_order)):
+                if (dn_order[n][0] == h and n < lead_all) or (last and n >= lead_all):
+                    end_send(dn_copy, dn_order, n)
 
         far_start(h)
 
@@ -499,34 +532,48 @@
         copy.wait()
     for copy in pending:
         copy.wait_send()
+    @pl.when(p == 0)
+    def _():
+        for h, j in up_order[-2:]:
+            up_copy(h, j).wait_send()
+
+    @pl.when(p == n_pts - 1)
+    def _():
+        for h, j in dn_order[-2:]:
+            dn_copy(h, j).wait_send()
+
     for h in range(HALVES):
         for j in range(n_pts):
-
             if j >= first_up:
 
-                @pl.when(p < j)
+                @pl.when((p > 0) & (p < j))
                 def _(h=h, j=j):
                     up_copy(h, j).wait_send()
 
             if j <= last_dn:
 
-                @pl.when(p > j)
+                @pl.when((p < n_pts - 1) & (p > j))
                 def _(h=h, j=j):
                     dn_copy(h, j).wait_send()
 
 
-def hand_over(upd_ref, prj_ref, upd_out, prj_out, sem):
-    copies = []
-    for i, (src, dst) in enumerate(((upd_ref, upd_out), (prj_ref, prj_out))):
+def hand_over(upd_ref, prj_ref, upd_out, prj_out, upd_held, prj_held, sem):
+    come, go = [], []
+    for i, (src, held, dst) in enumerate(
+        ((upd_ref, upd_held, upd_out), (prj_ref, prj_held, prj_out))
+    ):
         rows = src.shape[0] // PIECES
         for k in range(PIECES):
-            part = pl.ds(k * rows, rows)
-            copies.append(
-                pltpu.make_async_copy(src.at[part], dst.at[part], sem.at[i * PIECES + k])
-            )
-    for copy in copies:
+            some = pl.ds(k * rows, rows)
+            n = 2 * (i * PIECES + k)
+            come.append(pltpu.make_async_copy(src.at[some], held.at[some], sem.at[n]))
+            go.append(pltpu.make_async_copy(held.at[some], dst.at[some], sem.at[n + 1]))
+    for copy in come:
         copy.start()
-    for copy in copies:
+    for first, second in zip(come, go):
+        first.wait()
+        second.start()
+    for copy in go:
         copy.wait()
 
 
@@ -613,7 +660,11 @@
         ),
         in_specs=[hbm] * 2,
         out_specs=(hbm, hbm),
-        scratch_shapes=[dma((2 * PIECES,))],
+        scratch_shapes=[
+            pltpu.VMEM(updated.shape, BF16),
+            pltpu.VMEM(projection.shape, BF16),
+            dma((4 * PIECES,)),
+        ],
         compiler_params=pltpu.CompilerParams(vmem_limit_bytes=VMEM_BYTES),
     )(updated, projection)
 

time: 89.7 us -> 55.3 us (0.62)
  Pallas kernels: 88.9 us -> 54.5 us
    pallas_call x1, Pallas kernels: 32.9 us -> 2.08 us  [on_device(): pl.pallas_call(hand_over, out_shape=(jax.ShapeDtypeStruct(updated.shape,...]
    pallas_call x1, Pallas kernels: 55.9 us -> 52.4 us  [on_device(): pl.pallas_call(functools.partial(kernel, n_grid, n_pts, tile), out_shape=...]
where the time goes in v4:
time: 55.3 us; the launch traced here: 55.1 us
  Pallas kernels  54.5 us (99%)
  between operations  0.64 us (1%)
    pallas_call x1, Pallas kernels, on_device(): pl.pallas_call(functools.partial(kernel, n_grid, n_pts, tile), out_shape=...  52.4 us
    pallas_call x1, Pallas kernels, on_device(): pl.pallas_call(hand_over, out_shape=(jax.ShapeDtypeStruct(updated.shape,...  2.08 us

profile of v4, /device:TPU:0, one launch (start us, length us, event | category | flops | bytes accessed | tf_op | source)
XLA Modules:
  0.0 55.1 jit_solution(12076434537934630592)
XLA Ops:
  0.6 52.4 %shard_map.68 = (bf16[256,512]{1,0:T(8,128)(2,1)}, bf16[768,512]{1,0:T(8,128)(2,1)}) custom-call(bf16[256,512]{1,0:T(8,128)(2,1)} %orb_hbm.1, s32[1,4,24]{2,1,0:T(4,128)} %rows_hbm.1, s32[1,4]{1,0:T(1,128)} %count_hbm.1, bf16[384,768]{1,0:T(8,128)(2,1)} %bitcast.3, bf16[1024,768]{1,0:T(8,128)(2,1)} %fit_ref.1), custom_call_target="tpu_custom_call" | custom-call | flops 1409286144 | bytes 2162688 | tf_op jit(solution)/shard_map/pallas_call | solution.py:617
  53.0 2.1 %shard_map.69 = (bf16[256,512]{1,0:T(8,128)(2,1)}, bf16[768,512]{1,0:T(8,128)(2,1)}) custom-call(bf16[256,512]{1,0:T(8,128)(2,1)} %get-tuple-element.4.upd_ref, bf16[768,512]{1,0:T(8,128)(2,1)} %get-tuple-element.5.prj_ref), custom_call_target="tpu_custom_call" | custom-call | tf_op jit(solution)/shard_map/pallas_call | solution.py:655

commit v5 on v4

--- a/solution.py
+++ b/solution.py
@@ -11,7 +11,7 @@
 F32 = jnp.float32
 BF16 = jnp.bfloat16
 CORES = 2
-FAR = False
+FAR = True
 VMEM_BYTES = 63 << 20
 PIECES = 2
 HALVES = 2
@@ -407,13 +407,15 @@
         order += [n_pts - 1 - s, s]
     order += [j for j in range(n_pts) if j not in order]
     def far_first(js):
+        if far:
+            return [(h, j) for h in range(HALVES) for j in js]
         return [(h, j) for h in range(HALVES) for j in js[:-1]] + [
             (h, js[-1]) for h in range(HALVES)
         ]
 
     up_order = far_first(list(range(n_pts - 1, first_up - 1, -1)))
     dn_order = far_first(list(range(last_dn + 1)))
-    lead_all = HALVES * (n_pts - 1 - first_up)
+    lead_all = HALVES * (n_pts - first_up - (0 if far else 1))
 
     def end_send(copy_of, sequence, n):
         h, j = sequence[n]

time: 55.3 us -> 55.6 us (level)
  no operation moved by 1% of the time
where the time goes in v5:
time: 55.6 us; the launch traced here: 55.4 us
  Pallas kernels  54.8 us (99%)
  between operations  0.64 us (1%)
    pallas_call x1, Pallas kernels, on_device(): pl.pallas_call(functools.partial(kernel, n_grid, n_pts, tile), out_shape=...  52.7 us
    pallas_call x1, Pallas kernels, on_device(): pl.pallas_call(hand_over, out_shape=(jax.ShapeDtypeStruct(updated.shape,...  2.08 us

profile of v5, /device:TPU:0, one launch (start us, length us, event | category | flops | bytes accessed | tf_op | source)
XLA Modules:
  0.0 55.4 jit_solution(17999951134614135433)
XLA Ops:
  0.6 52.7 %shard_map.68 = (bf16[256,512]{1,0:T(8,128)(2,1)}, bf16[768,512]{1,0:T(8,128)(2,1)}) custom-call(bf16[256,512]{1,0:T(8,128)(2,1)} %orb_hbm.1, s32[1,4,24]{2,1,0:T(4,128)} %rows_hbm.1, s32[1,4]{1,0:T(1,128)} %count_hbm.1, bf16[384,768]{1,0:T(8,128)(2,1)} %bitcast.3, bf16[1024,768]{1,0:T(8,128)(2,1)} %fit_ref.1), custom_call_target="tpu_custom_call" | custom-call | flops 1409286144 | bytes 2162688 | tf_op jit(solution)/shard_map/pallas_call | solution.py:619
  53.3 2.1 %shard_map.69 = (bf16[256,512]{1,0:T(8,128)(2,1)}, bf16[768,512]{1,0:T(8,128)(2,1)}) custom-call(bf16[256,512]{1,0:T(8,128)(2,1)} %get-tuple-element.4.upd_ref, bf16[768,512]{1,0:T(8,128)(2,1)} %get-tuple-element.5.prj_ref), custom_call_target="tpu_custom_call" | custom-call | tf_op jit(solution)/shard_map/pallas_call | solution.py:657

commit v6 on v5

--- a/solution.py
+++ b/solution.py
@@ -14,7 +14,7 @@
 FAR = True
 VMEM_BYTES = 63 << 20
 PIECES = 2
-HALVES = 2
+CHUNKS = 4
 
 
 def kernel(
@@ -75,7 +75,7 @@
     sib = chip * CORES + (1 - core)
     cap = piece.shape[2]
     rows_dev, width = orb_ref.shape
-    half = width // HALVES
+    band = width // CHUNKS
     own_count = own.shape[0]
     block = n_pts * cap
     tiles = own_count // tile
@@ -297,7 +297,7 @@
     lax.fori_loop(0, tiles, term, 0)
 
     def bands(h):
-        return slice(h * half, (h + 1) * half)
+        return slice(h * band, (h + 1) * band)
 
     def sib_copy(h):
         return pltpu.make_async_remote_copy(
@@ -319,7 +319,7 @@
             device_id_type=MESH,
         )
 
-    for h in range(HALVES):
+    for h in range(CHUNKS):
 
         def product(b, carry, h=h):
             rows = pl.ds(pl.multiple_of(b * tile, tile), tile)
@@ -342,7 +342,7 @@
         return copies
 
     sent = []
-    for h in range(HALVES):
+    for h in range(CHUNKS):
         sib_copy(h).wait_recv()
         for r in range(1, chips):
             k = chip_at(r)
@@ -352,7 +352,7 @@
         sent = in_turn([chip_copy(h, r) for r in range(1, chips)], sent)
     pending += sent
     sent = []
-    for h in range(HALVES):
+    for h in range(CHUNKS):
         total = part[rows_of(g), bands(h)] + sib_in[h, chip].astype(F32)
         for r in range(1, chips):
             chip_copy(h, r).wait_recv()
@@ -373,14 +373,14 @@
             @pl.when(at_near)
             def _():
                 far_share_copy(h).wait_recv()
-                gather_start(proj_far.at[h], 1 + HALVES + h)
+                gather_start(proj_far.at[h], 1 + CHUNKS + h)
 
     def far_finish(h):
         if far:
 
             @pl.when(at_near)
             def _():
-                gather_finish(proj_far.at[h], 1 + HALVES + h)
+                gather_finish(proj_far.at[h], 1 + CHUNKS + h)
 
     def up_copy(h, j):
         return pltpu.make_async_remote_copy(
@@ -406,16 +406,10 @@
     for s in range(n_pts // 2):
         order += [n_pts - 1 - s, s]
     order += [j for j in range(n_pts) if j not in order]
-    def far_first(js):
-        if far:
-            return [(h, j) for h in range(HALVES) for j in js]
-        return [(h, j) for h in range(HALVES) for j in js[:-1]] + [
-            (h, js[-1]) for h in range(HALVES)
-        ]
-
-    up_order = far_first(list(range(n_pts - 1, first_up - 1, -1)))
-    dn_order = far_first(list(range(last_dn + 1)))
-    lead_all = HALVES * (n_pts - first_up - (0 if far else 1))
+    ups = range(n_pts - 1, first_up - 1, -1)
+    dns = range(last_dn + 1)
+    up_order = [(h, j) for j in ups for h in range(CHUNKS)]
+    dn_order = [(h, j) for j in dns for h in range(CHUNKS)]
 
     def end_send(copy_of, sequence, n):
         h, j = sequence[n]
@@ -424,68 +418,82 @@
         z_out[h, j] = exch[h, j].astype(BF16)
         copy_of(h, j).start()
 
-    for h in range(HALVES):
+    def relay_up(h, j):
+        @pl.when((p > 0) & (p < j))
+        def _():
+            up_copy(h, j).wait_recv()
+            z_out[h, j] = (exch[h, j] + z_in[h, j + 1].astype(F32)).astype(BF16)
+            up_copy(h, j).start()
+
+    def relay_dn(h, j):
+        @pl.when((p < n_pts - 1) & (p > j))
+        def _():
+            dn_copy(h, j).wait_recv()
+            z_out[h, j] = (exch[h, j] + z_in[h, j].astype(F32)).astype(BF16)
+            dn_copy(h, j).start()
+
+    lower = 2 * p < n_pts
+    lag = 2
+
+    def relays(first):
+        def one_side(near, near_order, other, other_order):
+            for n in range(max(len(near_order), len(other_order) + lag)):
+                if first <= n < len(near_order):
+                    near(*near_order[n])
+                if 0 <= n - lag + 1 < len(other_order) and n >= 1:
+                    other(*other_order[n - lag + 1])
+
+        @pl.when(lower)
+        def _():
+            one_side(relay_up, up_order, relay_dn, dn_order)
+
+        @pl.when(jnp.logical_not(lower))
+        def _():
+            one_side(relay_dn, dn_order, relay_up, up_order)
+
+    def near_relay(n):
+        @pl.when(lower)
+        def _():
+            relay_up(*up_order[n])
+
+        @pl.when(jnp.logical_not(lower))
+        def _():
+            relay_dn(*dn_order[n])
+
+    for h in range(CHUNKS):
         pending += gather_finish(proj.at[h], 1 + h)
         for j in order:
             exch[h, j] = jnp.dot(
                 fit[j * rows_dev : (j + 1) * rows_dev, :], proj[h], preferred_element_type=F32
             )
 
+        numbers = range(h, h + 1 if h < CHUNKS - 1 else len(up_order))
+
         @pl.when(p == 0)
-        def _(h=h, last=h == HALVES - 1):
-            for n in range(len(up_order)):
-                if (up_order[n][0] == h and n < lead_all) or (last and n >= lead_all):
-                    end_send(up_copy, up_order, n)
+        def _(numbers=numbers):
+            for n in numbers:
+                end_send(up_copy, up_order, n)
 
         @pl.when(p == n_pts - 1)
-        def _(h=h, last=h == HALVES - 1):
-            for n in range(len(dn_order)):
-                if (dn_order[n][0] == h and n < lead_all) or (last and n >= lead_all):
-                    end_send(dn_copy, dn_order, n)
-
+        def _(numbers=numbers):
+            for n in numbers:
+                end_send(dn_copy, dn_order, n)
+
+        if h >= lag:
+            near_relay(h - lag)
+
+    for h in range(CHUNKS):
         far_start(h)
-
     out_copies = []
-    for h in range(HALVES):
+    for h in range(CHUNKS):
         copy = pltpu.make_async_copy(proj.at[h], prj_hbm.at[:, bands(h)], out_sem.at[h])
         copy.start()
         out_copies.append(copy)
-    def relay_up(h, j):
-        @pl.when((p > 0) & (p < j))
-        def _():
-            up_copy(h, j).wait_recv()
-            z_out[h, j] = (exch[h, j] + z_in[h, j + 1].astype(F32)).astype(BF16)
-            up_copy(h, j).start()
-
-    def relay_dn(h, j):
-        @pl.when((p < n_pts - 1) & (p > j))
-        def _():
-            dn_copy(h, j).wait_recv()
-            z_out[h, j] = (exch[h, j] + z_in[h, j].astype(F32)).astype(BF16)
-            dn_copy(h, j).start()
-
-    lower = 2 * p < n_pts
-    ups = range(n_pts - 1, first_up - 1, -1)
-    dns = range(last_dn + 1)
-    for h in range(HALVES):
-
-        @pl.when(lower)
-        def _(h=h):
-            for j in ups:
-                relay_up(h, j)
-            for j in dns:
-                relay_dn(h, j)
-
-        @pl.when(jnp.logical_not(lower))
-        def _(h=h):
-            for j in dns:
-                relay_dn(h, j)
-            for j in ups:
-                relay_up(h, j)
-
+    relays(max(CHUNKS - lag, 0))
+    for h in range(CHUNKS):
         far_finish(h)
 
-    for h in range(HALVES):
+    for h in range(CHUNKS):
         if far:
 
             @pl.when(at_near)
@@ -508,7 +516,7 @@
 
         upd_ref[:, bands(h)] = (orb_ref[:, bands(h)].astype(F32) - exch[h, p]).astype(BF16)
         copy = pltpu.make_async_copy(
-            upd_ref.at[:, bands(h)], upd_hbm.at[:, bands(h)], out_sem.at[HALVES + h]
+            upd_ref.at[:, bands(h)], upd_hbm.at[:, bands(h)], out_sem.at[CHUNKS + h]
         )
         copy.start()
         out_copies.append(copy)
@@ -518,13 +526,13 @@
         @pl.when(at_end)
         def _():
             far_fit_copy().wait_send()
-            for h in range(HALVES):
+            for h in range(CHUNKS):
                 far_share_copy(h).wait_send()
 
         @pl.when(at_near)
         def _():
-            for h in range(HALVES):
-                tag = 1 + HALVES + h
+            for h in range(CHUNKS):
+                tag = 1 + CHUNKS + h
                 for r in range(chips):
                     gather_copy(proj_far.at[h], tag, r).wait_send()
                     if r > 0:
@@ -544,7 +552,7 @@
         for h, j in dn_order[-2:]:
             dn_copy(h, j).wait_send()
 
-    for h in range(HALVES):
+    for h in range(CHUNKS):
         for j in range(n_pts):
             if j >= first_up:
 
@@ -586,9 +594,9 @@
     own_count = n_grid * block
     col_count = n_pts * block
     chips = n_grid // CORES
-    half = width // HALVES
+    band = width // CHUNKS
     tile = next(t for t in (256, 128, own_count) if own_count % t == 0)
-    tags = 1 + 2 * HALVES
+    tags = 1 + 2 * CHUNKS
     pot_cols = jnp.transpose(potential, (1, 2, 0)).reshape(col_count, own_count)
     dma = pltpu.SemaphoreType.DMA
     buffers = [
@@ -598,21 +606,21 @@
         ((rows_dev, width), BF16),
         (fitted_basis.shape, BF16),
         ((rows_dev, own_count), BF16),
-        ((HALVES, own_count, half), BF16),
+        ((CHUNKS, own_count, band), BF16),
         ((2, col_count, tile), BF16),
         ((own_count, col_count), BF16),
         ((n_pts, n_pts, cap, width), BF16),
         ((col_count, width), BF16),
         ((own_count, width), BF16),
         ((own_count, width), F32),
-        ((HALVES, chips, block, half), BF16),
-        ((HALVES, chips, block, half), BF16),
-        ((HALVES, chips, block, half), BF16),
-        ((HALVES, chips, block, half), BF16),
-        ((HALVES, own_count, half), BF16),
-        ((HALVES, n_pts, rows_dev, half), F32),
-        ((HALVES, n_pts, rows_dev, half), BF16),
-        ((HALVES, n_pts + 1, rows_dev, half), BF16),
+        ((CHUNKS, chips, block, band), BF16),
+        ((CHUNKS, chips, block, band), BF16),
+        ((CHUNKS, chips, block, band), BF16),
+        ((CHUNKS, chips, block, band), BF16),
+        ((CHUNKS, own_count, band), BF16),
+        ((CHUNKS, n_pts, rows_dev, band), F32),
+        ((CHUNKS, n_pts, rows_dev, band), BF16),
+        ((CHUNKS, n_pts + 1, rows_dev, band), BF16),
     ]
     flops = 4 * own_count * col_count * width + 2 * fitted_basis.size * width
     hbm = pl.BlockSpec(memory_space=pl.ANY)
@@ -633,17 +641,17 @@
             dma((tags, chips)),
             dma((tags, chips)),
             dma((tags, chips)),
-            dma((HALVES,)),
-            dma((HALVES,)),
-            dma((HALVES, chips)),
-            dma((HALVES, chips)),
-            dma((HALVES, n_pts)),
-            dma((HALVES, n_pts)),
-            dma((HALVES, n_pts)),
-            dma((HALVES, n_pts)),
-            dma((1 + HALVES,)),
-            dma((1 + HALVES,)),
-            dma((2 * HALVES,)),
+            dma((CHUNKS,)),
+            dma((CHUNKS,)),
+            dma((CHUNKS, chips)),
+            dma((CHUNKS, chips)),
+            dma((CHUNKS, n_pts)),
+            dma((CHUNKS, n_pts)),
+            dma((CHUNKS, n_pts)),
+            dma((CHUNKS, n_pts)),
+            dma((1 + CHUNKS,)),
+            dma((1 + CHUNKS,)),
+            dma((2 * CHUNKS,)),
         ],
         compiler_params=pltpu.CompilerParams(
             collective_id=0,

time: 55.6 us -> 56.3 us (1.013); the launches traced: 55.4 us -> 55.4 us
  no operation moved by 1% of the time
where the time goes in v6:
time: 56.3 us; the launch traced here: 55.4 us
  Pallas kernels  54.8 us (97%)
  between operations  0.64 us (1%)
    pallas_call x1, Pallas kernels, on_device(): pl.pallas_call(functools.partial(kernel, n_grid, n_pts, tile), out_shape=...  52.7 us
    pallas_call x1, Pallas kernels, on_device(): pl.pallas_call(hand_over, out_shape=(jax.ShapeDtypeStruct(updated.shape,...  2.08 us

profile of v6, /device:TPU:0, one launch (start us, length us, event | category | flops | bytes accessed | tf_op | source)
XLA Modules:
  0.0 55.4 jit_solution(9237994670364180892)
XLA Ops:
  0.6 52.7 %shard_map.68 = (bf16[256,512]{1,0:T(8,128)(2,1)}, bf16[768,512]{1,0:T(8,128)(2,1)}) custom-call(bf16[256,512]{1,0:T(8,128)(2,1)} %orb_hbm.1, s32[1,4,24]{2,1,0:T(4,128)} %rows_hbm.1, s32[1,4]{1,0:T(1,128)} %count_hbm.1, bf16[384,768]{1,0:T(8,128)(2,1)} %bitcast.3, bf16[1024,768]{1,0:T(8,128)(2,1)} %fit_ref.1), custom_call_target="tpu_custom_call" | custom-call | flops 1409286144 | bytes 2162688 | tf_op jit(solution)/shard_map/pallas_call | solution.py:627
  53.3 2.1 %shard_map.69 = (bf16[256,512]{1,0:T(8,128)(2,1)}, bf16[768,512]{1,0:T(8,128)(2,1)}) custom-call(bf16[256,512]{1,0:T(8,128)(2,1)} %get-tuple-element.4.upd_ref, bf16[768,512]{1,0:T(8,128)(2,1)} %get-tuple-element.5.prj_ref), custom_call_target="tpu_custom_call" | custom-call | tf_op jit(solution)/shard_map/pallas_call | solution.py:665

commit v7 on v6

--- a/solution.py
+++ b/solution.py
@@ -11,10 +11,10 @@
 F32 = jnp.float32
 BF16 = jnp.bfloat16
 CORES = 2
-FAR = True
+FAR = False
 VMEM_BYTES = 63 << 20
 PIECES = 2
-CHUNKS = 4
+CHUNKS = 2
 
 
 def kernel(

time: 56.3 us -> 52.4 us (0.931); the launches traced: 55.4 us -> 52.2 us
  Pallas kernels: 54.8 us -> 51.6 us
    pallas_call x1, Pallas kernels: 52.7 us -> 49.5 us  [on_device(): pl.pallas_call(functools.partial(kernel, n_grid, n_pts, tile), out_shape=...]
where the time goes in v7:
time: 52.4 us; the launch traced here: 52.2 us
  Pallas kernels  51.6 us (98%)
  between operations  0.64 us (1%)
    pallas_call x1, Pallas kernels, on_device(): pl.pallas_call(functools.partial(kernel, n_grid, n_pts, tile), out_shape=...  49.5 us
    pallas_call x1, Pallas kernels, on_device(): pl.pallas_call(hand_over, out_shape=(jax.ShapeDtypeStruct(updated.shape,...  2.08 us

profile of v7, /device:TPU:0, one launch (start us, length us, event | category | flops | bytes accessed | tf_op | source)
XLA Modules:
  0.0 52.2 jit_solution(11115296437055773270)
XLA Ops:
  0.6 49.5 %shard_map.68 = (bf16[256,512]{1,0:T(8,128)(2,1)}, bf16[768,512]{1,0:T(8,128)(2,1)}) custom-call(bf16[256,512]{1,0:T(8,128)(2,1)} %orb_hbm.1, s32[1,4,24]{2,1,0:T(4,128)} %rows_hbm.1, s32[1,4]{1,0:T(1,128)} %count_hbm.1, bf16[384,768]{1,0:T(8,128)(2,1)} %bitcast.3, bf16[1024,768]{1,0:T(8,128)(2,1)} %fit_ref.1), custom_call_target="tpu_custom_call" | custom-call | flops 1409286144 | bytes 2162688 | tf_op jit(solution)/shard_map/pallas_call | solution.py:627
  50.1 2.1 %shard_map.69 = (bf16[256,512]{1,0:T(8,128)(2,1)}, bf16[768,512]{1,0:T(8,128)(2,1)}) custom-call(bf16[256,512]{1,0:T(8,128)(2,1)} %get-tuple-element.4.upd_ref, bf16[768,512]{1,0:T(8,128)(2,1)} %get-tuple-element.5.prj_ref), custom_call_target="tpu_custom_call" | custom-call | tf_op jit(solution)/shard_map/pallas_call | solution.py:665

commit v8 on v7

--- a/solution.py
+++ b/solution.py
@@ -11,7 +11,7 @@
 F32 = jnp.float32
 BF16 = jnp.bfloat16
 CORES = 2
-FAR = False
+FAR = True
 VMEM_BYTES = 63 << 20
 PIECES = 2
 CHUNKS = 2
@@ -440,6 +440,9 @@
             for n in range(max(len(near_order), len(other_order) + lag)):
                 if first <= n < len(near_order):
                     near(*near_order[n])
+                if n == lag:
+                    for h in range(CHUNKS):
+                        far_finish(h)
                 if 0 <= n - lag + 1 < len(other_order) and n >= 1:
                     other(*other_order[n - lag + 1])
 
@@ -490,8 +493,6 @@
         copy.start()
         out_copies.append(copy)
     relays(max(CHUNKS - lag, 0))
-    for h in range(CHUNKS):
-        far_finish(h)
 
     for h in range(CHUNKS):
         if far:

time: 52.4 us -> 52.9 us (level)
  no operation moved by 1% of the time
where the time goes in v8:
time: 52.9 us; the launch traced here: 52.7 us
  Pallas kernels  52.1 us (98%)
  between operations  0.64 us (1%)
    pallas_call x1, Pallas kernels, on_device(): pl.pallas_call(functools.partial(kernel, n_grid, n_pts, tile), out_shape=...  50 us
    pallas_call x1, Pallas kernels, on_device(): pl.pallas_call(hand_over, out_shape=(jax.ShapeDtypeStruct(updated.shape,...  2.08 us

profile of v8, /device:TPU:0, one launch (start us, length us, event | category | flops | bytes accessed | tf_op | source)
XLA Modules:
  0.0 52.7 jit_solution(16623167740231312000)
XLA Ops:
  0.6 50.0 %shard_map.68 = (bf16[256,512]{1,0:T(8,128)(2,1)}, bf16[768,512]{1,0:T(8,128)(2,1)}) custom-call(bf16[256,512]{1,0:T(8,128)(2,1)} %orb_hbm.1, s32[1,4,24]{2,1,0:T(4,128)} %rows_hbm.1, s32[1,4]{1,0:T(1,128)} %count_hbm.1, bf16[384,768]{1,0:T(8,128)(2,1)} %bitcast.3, bf16[1024,768]{1,0:T(8,128)(2,1)} %fit_ref.1), custom_call_target="tpu_custom_call" | custom-call | flops 1409286144 | bytes 2162688 | tf_op jit(solution)/shard_map/pallas_call | solution.py:628
  50.7 2.1 %shard_map.69 = (bf16[256,512]{1,0:T(8,128)(2,1)}, bf16[768,512]{1,0:T(8,128)(2,1)}) custom-call(bf16[256,512]{1,0:T(8,128)(2,1)} %get-tuple-element.4.upd_ref, bf16[768,512]{1,0:T(8,128)(2,1)} %get-tuple-element.5.prj_ref), custom_call_target="tpu_custom_call" | custom-call | tf_op jit(solution)/shard_map/pallas_call | solution.py:666
